TPU v7x, 1024 devices: a whole 8x8x8 slice. The times are simulated.
1024 devices in a mesh: node: 64 (over z, x), local: 16 (over y, core).
Axes of the slice: x: 8, y: 8, z: 8, core: 2. Of those that a mesh axis runs over, the one named last changes fastest.
Arguments:
- out_grad: bfloat16 [8192, 3584], P(('node', 'local')), may hold values from -6 to 6
- node_ids: int32 [8192, 4], P(('node', 'local')), may hold values from 0 to 63, as said below
- route_weights: bfloat16 [8192, 8], P(('node', 'local')), may hold values from 0.049804688 to 0.59765625
- saved_gate: bfloat16 [32768, 2048], P('node', 'local'), may hold values from -6 to 6
- saved_up: bfloat16 [32768, 2048], P('node', 'local'), may hold values from -6 to 6
- gate_weight: bfloat16 [3584, 131072], P(None, ('node', 'local')), may hold values from -0.1875 to 0.1875
- up_weight: bfloat16 [3584, 131072], P(None, ('node', 'local')), may hold values from -0.1875 to 0.1875
- down_weight: bfloat16 [131072, 3584], P(('node', 'local')), may hold values from -0.09375 to 0.09375
Outputs:
- in_grad: bfloat16 [8192, 3584], P(('node', 'local'))
Inputs may be any that keep to these rules, and one draw needn't show every extreme that they name: `node_ids`: each row names 4 different nodes. The 8 tokens of one device name each node at most 1 times in all, some node exactly 1 times; all tokens of the devices that share one index along local name each node exactly 4 * 8 times.
All inputs are finite; a program needn't handle non-finite values.
Results may differ from a plain program's by a relative error of at most 0.024.
Values may be sent and summed in bfloat16 or wider, within the bound.
A program may use at most 32 MiB of HBM per device.

v0:
```python
import jax
import jax.numpy as jnp
from jax import lax
from jax.sharding import PartitionSpec as P

EXP_NODE = 2


def shards(
    out_grad, node_ids, route_weights, saved_gate, saved_up, gate_weight, up_weight, down_weight
):
    token_count = out_grad.shape[0]
    width_model = out_grad.shape[1]
    pick_count = 4 * token_count
    node_count = lax.axis_size("node")
    slot_depth = max(1, pick_count // node_count)
    slot_count = node_count * slot_depth
    owner_count = lax.axis_size("local") // EXP_NODE
    own_slot = lax.axis_index("local") // owner_count
    slot_mask = (jnp.arange(EXP_NODE, dtype=jnp.int32) == own_slot).astype(jnp.float32)
    chosen = node_ids.reshape(pick_count)
    onehot = (chosen[:, None] == jnp.arange(node_count, dtype=jnp.int32)[None, :]).astype(jnp.int32)
    before = jnp.cumsum(onehot, axis=0) - onehot
    placing = jnp.sum(before * onehot, axis=1)
    target = chosen * slot_depth + placing
    select = (jnp.arange(slot_count, dtype=jnp.int32)[:, None] == target[None, :]).astype(
        jnp.bfloat16
    )
    repeated = jnp.repeat(out_grad, 4, axis=0)
    send_rows = jnp.dot(select, repeated, preferred_element_type=jnp.float32).astype(jnp.bfloat16)
    pick_gates = route_weights.reshape(pick_count, EXP_NODE)
    send_gates = jnp.dot(select, pick_gates, preferred_element_type=jnp.float32).astype(
        jnp.bfloat16
    )
    send_fill = jnp.sum(select.astype(jnp.float32), axis=1).astype(jnp.bfloat16)
    got_rows, got_gates, got_fill = (
        lax.all_to_all(
            send_rows.reshape(node_count, slot_depth, width_model),
            "node",
            split_axis=0,
            concat_axis=0,
            tiled=True,
        ),
        lax.all_to_all(
            send_gates.reshape(node_count, slot_depth, EXP_NODE),
            "node",
            split_axis=0,
            concat_axis=0,
            tiled=True,
        ),
        lax.all_to_all(
            send_fill.reshape(node_count, slot_depth),
            "node",
            split_axis=0,
            concat_axis=0,
            tiled=True,
        ),
    )
    got_rows = got_rows.reshape(slot_count, width_model)
    got_gates = got_gates.reshape(slot_count, EXP_NODE)
    fill_float = got_fill.reshape(slot_count).astype(jnp.float32)
    ranking = jnp.cumsum(fill_float) - 1.0
    compact = (
        (jnp.arange(pick_count, dtype=jnp.float32)[:, None] == ranking[None, :])
        & (fill_float[None, :] > 0.5)
    ).astype(jnp.bfloat16)
    compact_rows = jnp.dot(compact, got_rows, preferred_element_type=jnp.float32).astype(
        jnp.bfloat16
    )
    compact_gates = jnp.dot(compact, got_gates, preferred_element_type=jnp.float32).astype(
        jnp.bfloat16
    )
    piece = lax.all_gather((compact_rows, compact_gates), "local", axis=0, tiled=True)
    pre_gate = saved_gate.astype(jnp.float32)
    pre_up = saved_up.astype(jnp.float32)
    own_gate = jnp.sum(piece[1].astype(jnp.float32) * slot_mask[None, :], axis=1)
    projected = lax.dot_general(
        piece[0], down_weight, (((1,), (1,)), ((), ())), preferred_element_type=jnp.float32
    )
    hidden_grad = own_gate[:, None] * projected
    sigma_gate = jax.nn.sigmoid(pre_gate)
    d_gate = (hidden_grad * pre_up * sigma_gate * (1.0 + pre_gate * (1.0 - sigma_gate))).astype(
        jnp.bfloat16
    )
    d_up = (hidden_grad * pre_gate * sigma_gate).astype(jnp.bfloat16)
    gate_term = lax.dot_general(
        d_gate, gate_weight, (((1,), (1,)), ((), ())), preferred_element_type=jnp.float32
    )
    up_term = lax.dot_general(
        d_up, up_weight, (((1,), (1,)), ((), ())), preferred_element_type=jnp.float32
    )
    all_terms = gate_term + up_term
    summed = lax.psum_scatter(
        all_terms.astype(jnp.bfloat16), "local", scatter_dimension=0, tiled=True
    )
    returning = jnp.dot(compact.T, summed, preferred_element_type=jnp.float32).astype(jnp.bfloat16)
    returned = lax.all_to_all(
        returning.reshape(node_count, slot_depth, width_model),
        "node",
        split_axis=0,
        concat_axis=0,
        tiled=True,
    )
    per_pick = jnp.dot(
        select.T, returned.reshape(slot_count, width_model), preferred_element_type=jnp.float32
    )
    total_grad = jnp.sum(per_pick.reshape(token_count, 4, width_model), axis=1)
    return total_grad.astype(jnp.bfloat16)


def solution(mesh):
    return jax.shard_map(
        shards,
        mesh=mesh,
        in_specs=(
            P(("node", "local"), None),
            P(("node", "local"), None),
            P(("node", "local"), None),
            P("node", "local"),
            P("node", "local"),
            P(None, ("node", "local")),
            P(None, ("node", "local")),
            P(("node", "local"), None),
        ),
        out_specs=P(("node", "local"), None),
        check_vma=False,
    )
```

profile of v0, /device:TPU:49, one launch (start us, length us, event | category | flops | bytes accessed | tf_op | source)
XLA Modules:
  0.0 222.1 jit_solution(9685376603940669563)
XLA Ops:
  6.5 0.9 copy.42
  7.4 0.1 reshape.117
  7.5 0.1 fusion.22
  7.6 0.1 reduce_window_sum.18
  7.6 0.2 select_reduce_fusion
  7.8 0.1 fusion.28
  7.9 0.7 copy.43
  8.7 22.3 %all-to-all-start = ((bf16[64,1,1]{2,1,0:T(2,128)(2,1)}), bf16[64,1,1]{2,1,0:T(2,128)(2,1)S(1)}, u32[]{:S(2)}, u32[]{:S(2)}) async-start(bf16[64,1,1]{2,1,0:T(2,128)(2,1)} %copy.43), calls=%async_computation | async-start | bytes 65536 | tf_op jit(solution)/shard_map/all_to_all | solution.py:51
  31.0 0.9 broadcast_in_dim.2
  31.9 0.1 reshape.121
  32.0 0.4 fusion
  32.4 0.6 broadcast.56
  32.9 0.9 reduce.5
  33.8 0.9 reshape.134
  34.7 7.1 %all-to-all-done = bf16[64,1,1]{2,1,0:T(2,128)(2,1)S(1)} async-done(((bf16[64,1,1]{2,1,0:T(2,128)(2,1)}), bf16[64,1,1]{2,1,0:T(2,128)(2,1)S(1)}, u32[]{:S(2)}, u32[]{:S(2)}) %all-to-all-start) | async-done | bytes 160 | tf_op jit(solution)/shard_map/all_to_all | solution.py:51
  41.8 5.1 %all-to-all-start.2 = ((bf16[64,2,1792]{2,1,0:T(2,128)(2,1)}), bf16[64,2,1792]{2,1,0:T(2,128)(2,1)S(1)}, u32[]{:S(2)}, u32[]{:S(2)}) async-start(bf16[64,2,1792]{2,1,0:T(2,128)(2,1)} %reshape.134), calls=%async_computation.2 | async-start | bytes 917504 | tf_op jit(solution)/shard_map/all_to_all | solution.py:37
  46.9 0.0 all-gather.3.cloned.1.call-start
  46.9 0.1 reduce-window.8
  47.0 0.1 add_reduce_fusion
  47.2 1.2 compare_reduce_fusion
  48.4 13.4 %all-to-all-done.2 = bf16[64,2,1792]{2,1,0:T(2,128)(2,1)S(1)} async-done(((bf16[64,2,1792]{2,1,0:T(2,128)(2,1)}), bf16[64,2,1792]{2,1,0:T(2,128)(2,1)S(1)}, u32[]{:S(2)}, u32[]{:S(2)}) %all-to-all-start.2) | async-done | bytes 458784 | tf_op jit(solution)/shard_map/all_to_all | solution.py:37
  61.9 0.4 reshape.135
  62.2 0.9 convolution_convert_fusion.2
  63.2 0.1 reshape.118
  63.2 0.2 fusion.3
  63.4 0.8 copy.45
  64.2 7.1 %all-to-all-start.1 = ((bf16[64,1,2]{2,1,0:T(2,128)(2,1)}), bf16[64,1,2]{2,1,0:T(2,128)(2,1)S(1)}, u32[]{:S(2)}, u32[]{:S(2)}) async-start(bf16[64,1,2]{2,1,0:T(2,128)(2,1)} %copy.45), calls=%async_computation.1 | async-start | bytes 65536 | tf_op jit(solution)/shard_map/all_to_all | solution.py:44
  71.3 0.0 reduce-scatter.2.cloned.1.call-start
  71.4 10.7 %all-to-all-done.1 = bf16[64,1,2]{2,1,0:T(2,128)(2,1)S(1)} async-done(((bf16[64,1,2]{2,1,0:T(2,128)(2,1)}), bf16[64,1,2]{2,1,0:T(2,128)(2,1)S(1)}, u32[]{:S(2)}, u32[]{:S(2)}) %all-to-all-start.1) | async-done | bytes 288 | tf_op jit(solution)/shard_map/all_to_all | solution.py:44
  82.0 0.1 copy.46
  82.1 0.1 fusion.2
  82.3 18.8 %all-gather = bf16[16,32,2]{1,2,0:T(2,128)(2,1)S(1)} all-gather(bf16[1,32,2]{1,2,0:T(2,128)(2,1)S(1)} %fusion.2), channel_id=1, replica_groups=mesh['node'=64,'local'=16] {'local'}, dimensions={0}, use_global_device_ids=true | all-gather | bytes 2176 | tf_op jit(solution)/shard_map/all_gather | solution.py:73
  101.1 0.1 reshape.129
  101.2 0.1 multiply_reduce_fusion
  101.2 5.6 %all-gather.3.cloned.1.call-done = bf16[512,3584]{1,0:T(8,128)(2,1)} async-done(((bf16[32,3584]{1,0:T(8,128)(2,1)}), bf16[512,3584]{1,0:T(8,128)(2,1)}) %all-gather.3.cloned.1.call-update) | async-done | bytes 3670032 | tf_op jit(solution)/shard_map/all_gather | solution.py:73
  106.8 3.1 %convolution_multiply_fusion = f32[512,128]{1,0:T(8,128)S(1)} fusion(bf16[512,3584]{1,0:T(8,128)(2,1)} %all-gather.3.cloned.1.call-done, bf16[128,3584]{1,0:T(8,128)(2,1)S(1)} %copy-done.2, f32[512]{0:T(512)S(1)} %multiply_reduce_fusion), kind=kOutput, calls=%fused_computation.7 | convolution fusion | flops 469827584 | bytes 4851712 | tf_op jit(solution)/shard_map/dot_general | solution.py:77
  110.0 1.1 fusion.17
  111.2 0.0 copy-done.1
  111.2 2.9 %add_convert_fusion = bf16[512,3584]{1,0:T(8,128)(2,1)} fusion(f32[512,3584]{1,0:T(8,128)S(1)} %fusion.17, bf16[3584,128]{1,0:T(8,128)(2,1)S(1)} %copy-done.1, f32[512,128]{1,0:T(8,128)S(1)} %convolution_multiply_fusion, bf16[512,128]{1,0:T(8,128)(2,1)S(1)} %copy-done.3), kind=kOutput, calls=%fused_computation | convolution fusion | flops 473890816 | bytes 12320768 | tf_op jit(solution)/shard_map/dot_general | solution.py:89
  114.2 66.7 %reduce-scatter.2.cloned.1.call-done = bf16[32,3584]{1,0:T(8,128)(2,1)} async-done(((bf16[512,3584]{1,0:T(8,128)(2,1)}), bf16[32,3584]{1,0:T(8,128)(2,1)}) %reduce-scatter.2.cloned.1.call-update) | async-done | bytes 229392 | tf_op jit(solution)/shard_map/reduce_scatter | solution.py:93
  180.8 1.3 fusion.1
  182.1 0.9 reduce.6
  183.0 0.9 reshape.136
  183.9 13.7 %all-to-all-start.3 = ((bf16[64,2,1792]{2,1,0:T(2,128)(2,1)}), bf16[64,2,1792]{2,1,0:T(2,128)(2,1)S(1)}, u32[]{:S(2)}, u32[]{:S(2)}) async-start(bf16[64,2,1792]{2,1,0:T(2,128)(2,1)} %reshape.136), calls=%async_computation.4 | async-start | bytes 917504 | tf_op jit(solution)/shard_map/all_to_all | solution.py:97
  197.6 0.1 iota_compare_fusion.5
  197.6 16.4 %all-to-all-done.3 = bf16[64,2,1792]{2,1,0:T(2,128)(2,1)S(1)} async-done(((bf16[64,2,1792]{2,1,0:T(2,128)(2,1)}), bf16[64,2,1792]{2,1,0:T(2,128)(2,1)S(1)}, u32[]{:S(2)}, u32[]{:S(2)}) %all-to-all-start.3) | async-done | bytes 458784 | tf_op jit(solution)/shard_map/all_to_all | solution.py:97
  214.0 0.4 reshape.137
  214.4 0.9 convolution_reduce_fusion
  (17 shorter events, 0.1 us)
Async XLA Ops:
  6.5 103.5 %copy-start = (bf16[3584,128]{1,0:T(8,128)(2,1)S(1)}, bf16[3584,128]{1,0:T(8,128)(2,1)}, u32[]{:S(2)}) copy-start(bf16[3584,128]{1,0:T(8,128)(2,1)} %param.13) | copy-start | bytes 2752516
  6.5 56.6 %copy-start.5 = (bf16[8,8]{1,0:T(8,128)(2,1)S(1)}, bf16[8,8]{1,0:T(8,128)(2,1)}, u32[]{:S(2)}) copy-start(bf16[8,8]{1,0:T(8,128)(2,1)} %param.10) | copy-start | bytes 388
  6.5 100.3 %copy-start.2 = (bf16[128,3584]{1,0:T(8,128)(2,1)S(1)}, bf16[128,3584]{1,0:T(8,128)(2,1)}, u32[]{:S(2)}) copy-start(bf16[128,3584]{1,0:T(8,128)(2,1)} %param.15) | copy-start | bytes 2752516
  8.7 33.1 %all-to-all-start = ((bf16[64,1,1]{2,1,0:T(2,128)(2,1)}), bf16[64,1,1]{2,1,0:T(2,128)(2,1)S(1)}, u32[]{:S(2)}, u32[]{:S(2)}) async-start(bf16[64,1,1]{2,1,0:T(2,128)(2,1)} %copy.43), calls=%async_computation | async-start | bytes 65536 | tf_op jit(solution)/shard_map/all_to_all | solution.py:51
  41.8 20.1 %all-to-all-start.2 = ((bf16[64,2,1792]{2,1,0:T(2,128)(2,1)}), bf16[64,2,1792]{2,1,0:T(2,128)(2,1)S(1)}, u32[]{:S(2)}, u32[]{:S(2)}) async-start(bf16[64,2,1792]{2,1,0:T(2,128)(2,1)} %reshape.134), calls=%async_computation.2 | async-start | bytes 917504 | tf_op jit(solution)/shard_map/all_to_all | solution.py:37
  46.9 60.0 %all-gather.3.cloned.1.call-start = ((), (), s32[]{:S(2)}) async-start(), calls=%async_computation.5 | async-start | bytes 3899392 | tf_op jit(solution)/shard_map/all_gather | solution.py:73
  48.4 61.6 %copy-start.3 = (bf16[512,128]{1,0:T(8,128)(2,1)S(1)}, bf16[512,128]{1,0:T(8,128)(2,1)}, u32[]{:S(2)}) copy-start(bf16[512,128]{1,0:T(8,128)(2,1)} %param.11) | copy-start | bytes 393220
  48.4 61.6 %copy-start.4 = (bf16[512,128]{1,0:T(8,128)(2,1)S(1)}, bf16[512,128]{1,0:T(8,128)(2,1)}, u32[]{:S(2)}) copy-start(bf16[512,128]{1,0:T(8,128)(2,1)} %param.12) | copy-start | bytes 393220
  64.2 17.9 %all-to-all-start.1 = ((bf16[64,1,2]{2,1,0:T(2,128)(2,1)}), bf16[64,1,2]{2,1,0:T(2,128)(2,1)S(1)}, u32[]{:S(2)}, u32[]{:S(2)}) async-start(bf16[64,1,2]{2,1,0:T(2,128)(2,1)} %copy.45), calls=%async_computation.1 | async-start | bytes 65536 | tf_op jit(solution)/shard_map/all_to_all | solution.py:44
  71.3 109.5 %reduce-scatter.2.cloned.1.call-start = ((), (), s32[]{:S(2)}) async-start(), calls=%async_computation.6 | async-start | bytes 3899392 | tf_op jit(solution)/shard_map/reduce_scatter | solution.py:93
  110.0 1.2 copy-start.1
  183.9 30.2 %all-to-all-start.3 = ((bf16[64,2,1792]{2,1,0:T(2,128)(2,1)}), bf16[64,2,1792]{2,1,0:T(2,128)(2,1)S(1)}, u32[]{:S(2)}, u32[]{:S(2)}) async-start(bf16[64,2,1792]{2,1,0:T(2,128)(2,1)} %reshape.136), calls=%async_computation.4 | async-start | bytes 917504 | tf_op jit(solution)/shard_map/all_to_all | solution.py:97
Sparse Core Ops, SparseCore 0:
  63.3 43.5 all-gather.2
  114.3 66.4 reduce-scatter.1
where the time goes:
time: 223 us; the launch traced here: 222 us
  waiting for transfers between devices  120 us (54%)
  starting transfers between devices  48.3 us (22%)
  blocking collectives  18.8 us (8%)
  between operations  13.6 us (6%)
  matrix products  11 us (5%)
  local copies, waits for them, and re-layouts  6.76 us (3%)
  other arithmetic  3.83 us (2%)
    reduce_scatter x1, waiting for transfers between devices, shards(): lax.psum_scatter(all_terms.astype(jnp.bfloat16), 'local', scatter_dimensi...  66.7 us
    all_to_all x1, starting transfers between devices, shards(): lax.all_to_all(send_fill.reshape(node_count, slot_depth), 'node', split_a...  22.3 us
    all_gather x1, blocking collectives, shards(): lax.all_gather((compact_rows, compact_gates), 'local', axis=0, tiled=True)  18.8 us
    all_to_all x1, waiting for transfers between devices, shards(): lax.all_to_all(returning.reshape(node_count, slot_depth, width_model), 'n...  16.4 us
    all_to_all x1, starting transfers between devices, shards(): lax.all_to_all(returning.reshape(node_count, slot_depth, width_model), 'n...  13.7 us
    all_to_all x1, waiting for transfers between devices, shards(): lax.all_to_all(send_rows.reshape(node_count, slot_depth, width_model), 'n...  13.4 us
    all_to_all x1, waiting for transfers between devices, shards(): lax.all_to_all(send_gates.reshape(node_count, slot_depth, EXP_NODE), 'nod...  10.7 us
    all_to_all x1, starting transfers between devices, shards(): lax.all_to_all(send_gates.reshape(node_count, slot_depth, EXP_NODE), 'nod...  7.1 us
  transfers between devices with their start and end apart: 6, of which 6 were waited for; matrix products, arithmetic and copies ran while one was open for 3% of the time, Pallas kernels for 0%

commit v1 on v0

v1 whole, which is shorter than its diff:
```python
import functools

import jax
import jax.numpy as jnp
from jax import lax
from jax.experimental import pallas as pl
from jax.experimental.pallas import tpu as pltpu
from jax.sharding import PartitionSpec as P

MESH = pl.DeviceIdType.MESH
F32 = jnp.float32
BF16 = jnp.bfloat16
LANE = 128
SUB = 16
CHUNKS = 2


def iota(shape, dim):
    return lax.broadcasted_iota(jnp.int32, shape, dim)


def one_hot(cond):
    return jnp.where(cond, 1.0, 0.0).astype(BF16)


def dot_nn(a, b):
    return lax.dot_general(a, b, (((1,), (0,)), ((), ())), preferred_element_type=F32)


def dot_nt(a, b):
    return lax.dot_general(a, b, (((1,), (1,)), ((), ())), preferred_element_type=F32)


def kernel(
    cfg,
    og_ref,
    ids_ref,
    rw_ref,
    sg_hbm,
    su_hbm,
    wg_hbm,
    wu_hbm,
    wd_hbm,
    out_ref,
    sg,
    su,
    wd,
    wgu,
    tx,
    rx,
    tx2,
    rx2,
    x0,
    x1,
    pack_t,
    hacc,
    hid,
    part,
    rsib,
    chain_start,
    chain,
    load_sem,
    out_send,
    out_recv,
    back_send,
    back_recv,
    ag_send,
    ag_recv,
    sib_send,
    sib_recv,
    psib_send,
    psib_recv,
    rs_send,
    rs_recv,
):
    nodes, ring, toks, picks, tiles = cfg
    half = ring // 2
    rows = toks * picks
    slots = nodes * SUB
    packed = SUB * rows
    width = tiles * LANE
    xs = (x0, x1)

    node = lax.axis_index("node")
    local = lax.axis_index("local")
    y = local // 2
    core = local % 2
    right = ((y + 1) % ring) * 2 + core
    left = ((y + ring - 1) % ring) * 2 + core
    sibling = y * 2 + (1 - core)

    order = [half]
    for s in range(half - 1, 0, -1):
        order += [s, -s]
    order.append(0)

    def pos(d):
        return order.index(half if d == -half else d)

    streams = ((1, 0, half), (1, 1, half - 1), (-1, 0, half - 1), (-1, 1, half))

    barrier = pltpu.get_barrier_semaphore()

    def greet(i, carry):
        peer = (node + i) % nodes
        pl.semaphore_signal(barrier, inc=1, device_id=(peer, local), device_id_type=MESH)
        return carry

    lax.fori_loop(1, nodes, greet, 0)
    for who in (right, left, sibling):
        pl.semaphore_signal(barrier, inc=1, device_id=(node, who), device_id_type=MESH)

    loads = [
        pltpu.make_async_copy(wd_hbm, wd, load_sem.at[0]),
        pltpu.make_async_copy(sg_hbm, sg, load_sem.at[1]),
        pltpu.make_async_copy(su_hbm, su, load_sem.at[2]),
        pltpu.make_async_copy(wg_hbm, wgu.at[:, pl.ds(0, LANE)], load_sem.at[3]),
        pltpu.make_async_copy(wu_hbm, wgu.at[:, pl.ds(LANE, LANE)], load_sem.at[4]),
    ]
    for load in loads:
        load.start()

    with jax.named_scope("fill_slots"):
        idf = ids_ref[...].astype(F32)
        gates = rw_ref[...].astype(F32)
        lane8 = iota((toks, LANE), 1)
        tok8 = iota((toks, LANE), 0)
        ids_lane = [
            jnp.sum(
                jnp.where(lane8 % toks == tok8, idf[:, j : j + 1], 0.0), axis=0, keepdims=True
            ).astype(jnp.int32)
            for j in range(picks)
        ]
        lane1 = iota((1, LANE), 1)
        slot_row = iota((slots, LANE), 0)
        hit = None
        for j in range(picks):
            key = ids_lane[j] * SUB + lane1 // toks
            same = slot_row == key
            hit = same if hit is None else hit | same
        spread = one_hot(hit)
        pick_key = jnp.full((1, LANE), -1, jnp.int32)
        for j in range(picks):
            mine = ((lane1 // toks) % picks == j) & (lane1 < 2 * rows)
            pick_key = jnp.where(mine, ids_lane[j] * SUB + (SUB - 2) + lane1 // rows, pick_key)
        spread_meta = one_hot(slot_row == pick_key)
        meta = [
            jnp.where(
                lane8 < LANE // 2,
                gates[:, 2 * j : 2 * j + 1],
                gates[:, 2 * j + 1 : 2 * j + 2],
            )
            for j in range(picks)
        ]
        meta = jnp.concatenate(
            meta + [jnp.ones((rows, LANE), F32), jnp.zeros((LANE - 2 * rows, LANE), F32)], axis=0
        ).astype(BF16)
        meta_slots = dot_nn(spread_meta, meta)
        grads = og_ref[...].astype(F32)
        for c in range(CHUNKS):
            stack = [
                grads[:, c * width + k * LANE : c * width + (k + 1) * LANE] for k in range(tiles)
            ]
            stack.append(jnp.zeros((LANE - tiles * toks, LANE), F32))
            block = dot_nn(spread, jnp.concatenate(stack, axis=0).astype(BF16))
            if c == 0:
                block = block + meta_slots
            tx[c] = block.astype(BF16).reshape(nodes, SUB, LANE)
            rx[c, node] = tx[c, node]

    pl.semaphore_wait(barrier, nodes - 1 + 3)

    def to_node(src, dst, send_sem, recv_sem, c):
        def go(i, carry):
            peer = (node + i) % nodes
            pltpu.make_async_remote_copy(
                src_ref=src.at[c, peer],
                dst_ref=dst.at[c, node],
                send_sem=send_sem.at[c],
                recv_sem=recv_sem.at[c],
                device_id=(peer, local),
                device_id_type=MESH,
            ).start()
            return carry

        lax.fori_loop(1, nodes, go, 0)

    def all_of(src, dst, send_sem, recv_sem, c):
        return pltpu.make_async_remote_copy(
            src_ref=src.at[c, pl.ds(0, nodes - 1)],
            dst_ref=dst.at[c, pl.ds(0, nodes - 1)],
            send_sem=send_sem.at[c],
            recv_sem=recv_sem.at[c],
            device_id=(node, sibling),
            device_id_type=MESH,
        )

    for c in range(CHUNKS):
        to_node(tx, rx, out_send, out_recv, c)

    def ag(c, st, s):
        way, h, _ = streams[st]
        return pltpu.make_async_remote_copy(
            src_ref=xs[c].at[pos(-way * (s - 1)), 0, h],
            dst_ref=xs[c].at[pos(-way * s), 0, h],
            send_sem=ag_send.at[c, st, s - 1],
            recv_sem=ag_recv.at[c, st, s - 1],
            device_id=(node, right if way > 0 else left),
            device_id_type=MESH,
        )

    def to_sibling(c, p, h):
        return pltpu.make_async_remote_copy(
            src_ref=xs[c].at[p, 0, h],
            dst_ref=xs[c].at[p, 1, h],
            send_sem=sib_send.at[c, p, h],
            recv_sem=sib_recv.at[c, p, h],
            device_id=(node, sibling),
            device_id_type=MESH,
        )

    def ag_start(c):
        for st in range(4):
            if streams[st][2] > 0:
                ag(c, st, 1).start()
        for h in range(2):
            to_sibling(c, pos(0), h).start()

    def ag_step(c, s):
        for st in (0, 3, 1, 2):
            way, h, hops = streams[st]
            if s <= hops:
                ag(c, st, s).wait_recv()
                if s < hops:
                    ag(c, st, s + 1).start()
                to_sibling(c, pos(-way * s), h).start()

    def sib_wait(c, ps):
        for p in ps:
            for h in range(2):
                to_sibling(c, p, h).wait_recv()

    def fill_key():
        flat = rx[0].reshape(slots, LANE)
        first = one_hot(iota((SUB, LANE), 1) == 0)
        lane_s = iota((SUB, slots), 1)
        flag = jnp.where(lane_s % SUB == SUB - 1, dot_nt(first, flat), 0.0).astype(BF16)
        owner = one_hot(iota((slots, LANE), 0) // SUB == iota((slots, LANE), 1))
        by_node = dot_nn(flag, owner).astype(BF16)
        below = one_hot(iota((LANE, slots), 0) <= iota((LANE, slots), 1) // SUB)
        equal = one_hot(iota((LANE, slots), 0) == iota((LANE, slots), 1) // SUB)
        count = dot_nn(by_node, below)[0:1]
        filled = dot_nn(by_node, equal)[0:1]
        lane = iota((1, slots), 1)
        key = (lane % SUB) * rows + count.astype(jnp.int32) - 1
        return jnp.where(filled > 0.5, key, -1)

    def fill_key_rows():
        flat = rx[0].reshape(slots, LANE)
        take = one_hot(iota((LANE, slots), 1) == iota((LANE, slots), 0) * SUB + SUB - 1)
        by_node = dot_nn(take, flat).astype(BF16)
        below = one_hot(iota((slots, LANE), 1) <= iota((slots, LANE), 0) // SUB)
        equal = one_hot(iota((slots, LANE), 1) == iota((slots, LANE), 0) // SUB)
        count = dot_nn(below, by_node)
        filled = dot_nn(equal, by_node)
        key = (iota((slots, LANE), 0) % SUB) * rows + count.astype(jnp.int32) - 1
        return jnp.where(filled > 0.5, key, -1)

    def compact(c, pack):
        got = dot_nn(pack, rx[c].reshape(slots, LANE)).astype(BF16)
        for k in range(tiles + (1 if c == 0 else 0)):
            src = k if k < tiles else SUB - 2
            xs[c][pos(0), 0, :, :, k * LANE : (k + 1) * LANE] = got[
                src * rows : (src + 1) * rows
            ].reshape(2, rows // 2, LANE)

    def project(c, p0, p1):
        lhs = xs[c][p0:p1, :, :, :, 0:width].reshape((p1 - p0) * 2 * rows, width)
        value = dot_nt(lhs, wd[:, c * width : (c + 1) * width])
        span = pl.ds(p0 * 2 * rows, (p1 - p0) * 2 * rows)
        if c == 0:
            hacc[span, :] = value
        else:
            hacc[span, :] = hacc[span, :] + value

    own_slot = local // (ring * 2 // 2)

    def activate(p0, p1):
        for p in range(p0, p1):
            for who in range(2):
                src_core = core if who == 0 else 1 - core
                src = ((y + order[p] + ring) % ring) * 2 + src_core
                a = sg[src].astype(F32)
                b = su[src].astype(F32)
                g = xs[0][p, who, :, :, width : width + LANE].reshape(rows, LANE).astype(F32)
                gate = jnp.where(own_slot == 0, g[:, 0:1], g[:, LANE // 2 : LANE // 2 + 1])
                base = (p * 2 + who) * rows
                grad = gate * hacc[base : base + rows, :]
                sig = 1.0 / (1.0 + jnp.exp(-a))
                hid[p, who, :, 0:LANE] = (grad * b * sig * (1.0 + a * (1.0 - sig))).astype(BF16)
                hid[p, who, :, LANE : 2 * LANE] = (grad * a * sig).astype(BF16)

    def psib(c, p):
        return pltpu.make_async_remote_copy(
            src_ref=part.at[c, p, 1],
            dst_ref=rsib.at[c, p],
            send_sem=psib_send.at[c, p],
            recv_sem=psib_recv.at[c, p],
            device_id=(node, sibling),
            device_id_type=MESH,
        )

    step_cols = 2 * LANE if width % (2 * LANE) == 0 else LANE

    def expand(c, p0, p1):
        lhs = hid[p0:p1].reshape((p1 - p0) * 2 * rows, 2 * LANE)
        for n in range(0, width, step_cols):
            value = dot_nt(lhs, wgu[c * width + n : c * width + n + step_cols, :])
            part[c, p0:p1, :, :, :, n : n + step_cols] = value.astype(BF16).reshape(
                p1 - p0, 2, 2, rows // 2, step_cols
            )
        for p in range(p0, p1):
            psib(c, p).start()

    def chip_sum(c, p, h):
        return part[c, p, 0, h].astype(F32) + rsib[c, p, h].astype(F32)

    def rs(c, st, s):
        way = streams[st][0]
        return pltpu.make_async_remote_copy(
            src_ref=chain_start.at[c, st] if s == 1 else chain.at[c, st, s - 2],
            dst_ref=chain.at[c, st, s - 1],
            send_sem=rs_send.at[c, st, s - 1],
            recv_sem=rs_recv.at[c, st, s - 1],
            device_id=(node, right if way > 0 else left),
            device_id_type=MESH,
        )

    def rs_start(c):
        for p in range(3):
            psib(c, p).wait_recv()
        for st in (0, 3, 1, 2):
            way, h, hops = streams[st]
            chain_start[c, st] = chip_sum(c, pos(way * hops), h).astype(BF16)
            rs(c, st, 1).start()

    def rs_step(c, s):
        for st in (0, 3, 1, 2):
            way, h, hops = streams[st]
            if s < hops:
                rs(c, st, s).wait_recv()
                total = chain[c, st, s - 1].astype(F32) + chip_sum(c, pos(way * (hops - s)), h)
                chain[c, st, s - 1] = total.astype(BF16)
                rs(c, st, s + 1).start()

    def rs_finish(c):
        sums = []
        for h in range(2):
            total = chip_sum(c, pos(0), h)
            for st in range(4):
                way, sh, hops = streams[st]
                if sh == h:
                    rs(c, st, hops).wait_recv()
                    total = total + chain[c, st, hops - 1].astype(F32)
            sums.append(total)
        total = jnp.concatenate(sums, axis=0).astype(BF16)
        stack = [total[:, k * LANE : (k + 1) * LANE] for k in range(tiles)]
        stack.append(jnp.zeros(((SUB - tiles) * rows, LANE), BF16))
        back = dot_nn(pack_t[...], jnp.concatenate(stack, axis=0))
        tx2[c] = back.astype(BF16).reshape(nodes, SUB, LANE)
        rx2[c, node] = tx2[c, node]
        to_node(tx2, rx2, back_send, back_recv, c)

    def combine(c, merge):
        all_of(tx2, rx2, back_send, back_recv, c).wait_recv()
        got = dot_nn(merge, rx2[c].reshape(slots, LANE))
        for k in range(tiles):
            out_ref[:, c * width + k * LANE : c * width + (k + 1) * LANE] = got[
                k * toks : (k + 1) * toks
            ].astype(BF16)

    all_of(tx, rx, out_send, out_recv, 0).wait_recv()
    with jax.named_scope("compact"):
        key = fill_key()
        pack = one_hot(iota((packed, slots), 0) == key)
        compact(0, pack)
    ag_start(0)
    with jax.named_scope("unpack_matrix"):
        key_rows = fill_key_rows()
        for q in range(packed // LANE):
            pack_t[:, q * LANE : (q + 1) * LANE] = one_hot(
                key_rows == iota((slots, LANE), 1) + q * LANE
            )
    for load in loads:
        load.wait()
    ag_step(0, 1)
    all_of(tx, rx, out_send, out_recv, 1).wait_recv()
    with jax.named_scope("compact"):
        compact(1, pack)
    ag_start(1)
    last = len(order) - 1

    def pair(s):
        return (0, 1) if s == half else (pos(s), pos(-s) + 1) if s else (last, last + 1)

    for s in range(1, half + 1):
        if s < half:
            ag_step(0, s + 1)
        ag_step(1, s)
        p0, p1 = pair(s - 1)
        for c in range(CHUNKS):
            sib_wait(c, range(p0, p1))
            project(c, p0, p1)
        activate(p0, p1)
    p0, p1 = pair(half)
    for c in range(CHUNKS):
        sib_wait(c, range(p0, p1))
        project(c, p0, p1)
    activate(p0, p1)

    expand(0, 0, 3)
    rs_start(0)
    expand(1, 0, 3)
    rs_start(1)
    expand(0, 3, last + 1)
    for p in range(3, last + 1):
        psib(0, p).wait_recv()
    rs_step(0, 1)
    expand(1, 3, last + 1)
    for p in range(3, last + 1):
        psib(1, p).wait_recv()
    rs_step(1, 1)
    for s in range(2, half):
        for c in range(CHUNKS):
            rs_step(c, s)
    for c in range(CHUNKS):
        rs_finish(c)
    with jax.named_scope("merge_matrix"):
        spot = iota((LANE, nodes * SUB), 1)
        tok_row = one_hot(iota((LANE, toks), 0) % toks == iota((LANE, toks), 1))
        ids_rows = dot_nn(tok_row, idf.astype(BF16)).astype(jnp.int32)
        row_tile = iota((LANE, 1), 0) // toks
        hit = None
        for j in range(picks):
            same = spot == ids_rows[:, j : j + 1] * SUB + row_tile
            hit = same if hit is None else hit | same
        merge = one_hot(hit)
    for c in range(CHUNKS):
        combine(c, merge)

    for c in range(CHUNKS):
        all_of(tx, rx, out_send, out_recv, c).wait_send()
        all_of(tx2, rx2, back_send, back_recv, c).wait_send()
        for st in range(4):
            for s in range(1, streams[st][2] + 1):
                ag(c, st, s).wait_send()
                rs(c, st, s).wait_send()
        for p in range(last + 1):
            for h in range(2):
                to_sibling(c, p, h).wait_send()
            psib(c, p).wait_send()


def layer(cfg, og, ids, rw, sg, su, wg, wu, wd):
    nodes, ring, toks, picks, tiles = cfg
    half = ring // 2
    rows = toks * picks
    width = tiles * LANE
    slots = nodes * SUB
    piece = rows // 2
    dma = pltpu.SemaphoreType.DMA
    sg = sg.reshape(2 * ring, rows, LANE)
    su = su.reshape(2 * ring, rows, LANE)
    in_vmem = pl.BlockSpec(memory_space=pltpu.VMEM)
    anywhere = pl.BlockSpec(memory_space=pl.ANY)
    return pl.pallas_call(
        functools.partial(kernel, cfg),
        out_shape=jax.ShapeDtypeStruct(og.shape, BF16),
        in_specs=[in_vmem] * 3 + [anywhere] * 5,
        out_specs=in_vmem,
        scratch_shapes=[
            pltpu.VMEM(sg.shape, BF16),
            pltpu.VMEM(su.shape, BF16),
            pltpu.VMEM(wd.shape, BF16),
            pltpu.VMEM((wg.shape[0], 2 * LANE), BF16),
            pltpu.VMEM((CHUNKS, nodes, SUB, LANE), BF16),
            pltpu.VMEM((CHUNKS, nodes, SUB, LANE), BF16),
            pltpu.VMEM((CHUNKS, nodes, SUB, LANE), BF16),
            pltpu.VMEM((CHUNKS, nodes, SUB, LANE), BF16),
            pltpu.VMEM((ring, 2, 2, piece, width + LANE), BF16),
            pltpu.VMEM((ring, 2, 2, piece, width), BF16),
            pltpu.VMEM((slots, SUB * rows), BF16),
            pltpu.VMEM((ring * 2 * rows, LANE), F32),
            pltpu.VMEM((ring, 2, rows, 2 * LANE), BF16),
            pltpu.VMEM((CHUNKS, ring, 2, 2, piece, width), BF16),
            pltpu.VMEM((CHUNKS, ring, 2, piece, width), BF16),
            pltpu.VMEM((CHUNKS, 4, piece, width), BF16),
            pltpu.VMEM((CHUNKS, 4, half, piece, width), BF16),
            dma((5,)),
            dma((CHUNKS,)),
            dma((CHUNKS,)),
            dma((CHUNKS,)),
            dma((CHUNKS,)),
            dma((CHUNKS, 4, half)),
            dma((CHUNKS, 4, half)),
            dma((CHUNKS, ring, 2)),
            dma((CHUNKS, ring, 2)),
            dma((CHUNKS, ring)),
            dma((CHUNKS, ring)),
            dma((CHUNKS, 4, half)),
            dma((CHUNKS, 4, half)),
        ],
        compiler_params=pltpu.CompilerParams(
            collective_id=0, has_side_effects=True, vmem_limit_bytes=48 * 1024 * 1024
        ),
    )(og, ids, rw, sg, su, wg, wu, wd)


def solution(mesh):
    nodes = mesh.shape["node"]
    ring = mesh.shape["local"] // 2

    def shards(og, ids, rw, sg, su, wg, wu, wd):
        toks, model = og.shape
        cfg = (nodes, ring, toks, ids.shape[1], model // (CHUNKS * LANE))
        return layer(cfg, og, ids, rw, sg, su, wg, wu, wd)

    return jax.shard_map(
        shards,
        mesh=mesh,
        in_specs=(
            P(("node", "local"), None),
            P(("node", "local"), None),
            P(("node", "local"), None),
            P("node", "local"),
            P("node", "local"),
            P(None, ("node", "local")),
            P(None, ("node", "local")),
            P(("node", "local"), None),
        ),
        out_specs=P(("node", "local"), None),
        check_vma=False,
    )
```

time: 223 us -> 110 us (0.49)
  the two profiles are of different devices: /device:TPU:49 before, /device:TPU:1 now
where the time goes in v1:
time: 110 us
  Pallas kernels  102 us (93%)
  local copies, waits for them, and re-layouts  8.15 us (7%)
    pallas_call x1, Pallas kernels, layer(): pl.pallas_call(functools.partial(kernel, cfg), out_shape=jax.ShapeDtypeSt...  102 us
    unnamed x18, local copies, waits for them, and re-layouts  8.15 us

profile of v1, /device:TPU:1, one launch (start us, length us, event | category | flops | bytes accessed | tf_op | source)
XLA Modules:
  0.0 110.0 jit_solution(15901661037746370118)
XLA Ops:
  0.0 0.0 copy-start.7
  0.0 0.7 copy-done.7
  0.7 0.0 copy-start.6
  0.7 0.1 copy.9.ids_ref
  0.8 0.6 copy-done.6
  1.4 0.0 copy-start
  1.4 1.2 %copy-done = bf16[3584,128]{1,0:T(8,128)(2,1)S(1)} copy-done((bf16[3584,128]{1,0:T(8,128)(2,1)S(1)}, bf16[3584,128]{1,0:T(8,128)(2,1)}, u32[]{:S(2)}) %copy-start) | copy-done | bytes 917528
  2.5 0.0 copy-start.1
  2.5 1.2 %copy-done.1 = bf16[3584,128]{1,0:T(8,128)(2,1)S(1)} copy-done((bf16[3584,128]{1,0:T(8,128)(2,1)S(1)}, bf16[3584,128]{1,0:T(8,128)(2,1)}, u32[]{:S(2)}) %copy-start.1) | copy-done | bytes 917528
  3.7 0.0 copy-start.2
  3.7 1.2 %copy-done.2 = bf16[128,3584]{1,0:T(8,128)(2,1)S(1)} copy-done((bf16[128,3584]{1,0:T(8,128)(2,1)S(1)}, bf16[128,3584]{1,0:T(8,128)(2,1)}, u32[]{:S(2)}) %copy-start.2) | copy-done | bytes 917528
  4.9 0.0 copy-start.3
  4.9 0.9 copy-done.3
  5.8 0.0 copy-start.4
  5.8 0.9 copy-done.4
  6.7 0.0 copy-start.5
  6.7 0.8 copy-done.5
  7.5 101.8 %shard_map.82 = bf16[8,3584]{1,0:T(8,128)(2,1)S(1)} custom-call(bf16[8,3584]{1,0:T(8,128)(2,1)S(1)} %copy-done.5, s32[8,4]{1,0:T(8,128)S(1)} %copy.9.ids_ref, bf16[8,8]{1,0:T(8,128)(2,1)S(1)} %copy-done.6, bf16[16,32,128]{2,1,0:T(8,128)(2,1)S(1)} %bitcast.2, bf16[16,32,128]{2,1,0:T(8,128)(2,1)S(1)} %bitcast.3, bf16[3584,128]{1,0:T(8,128)(2,1)S(1)} %copy-done, ...), custom_call_target="tpu_custom_call" | custom-call | tf_op jit(solution)/shard_map/pallas_call | solution.py:476
  109.4 0.6 copy.11
Async XLA Ops:
  0.0 0.7 copy-start.7
  0.7 0.7 copy-start.6
  1.4 1.2 %copy-start = (bf16[3584,128]{1,0:T(8,128)(2,1)S(1)}, bf16[3584,128]{1,0:T(8,128)(2,1)}, u32[]{:S(2)}) copy-start(bf16[3584,128]{1,0:T(8,128)(2,1)} %wg_hbm.1) | copy-start | bytes 2752516
  2.5 1.2 %copy-start.1 = (bf16[3584,128]{1,0:T(8,128)(2,1)S(1)}, bf16[3584,128]{1,0:T(8,128)(2,1)}, u32[]{:S(2)}) copy-start(bf16[3584,128]{1,0:T(8,128)(2,1)} %wu_hbm.1) | copy-start | bytes 2752516
  3.7 1.2 %copy-start.2 = (bf16[128,3584]{1,0:T(8,128)(2,1)S(1)}, bf16[128,3584]{1,0:T(8,128)(2,1)}, u32[]{:S(2)}) copy-start(bf16[128,3584]{1,0:T(8,128)(2,1)} %wd_hbm.1) | copy-start | bytes 2752516
  4.9 0.9 copy-start.3
  5.8 0.9 copy-start.4
  6.7 0.8 copy-start.5

commit v2 on v1

--- a/solution.py
+++ b/solution.py
@@ -1,4 +1,5 @@
 import functools
+import math
 
 import jax
 import jax.numpy as jnp
@@ -13,6 +14,10 @@
 LANE = 128
 SUB = 16
 CHUNKS = 2
+PARTS = 1
+C1_AFTER = 0
+RS_LAG = 2
+VMEM_BYTES = 63 * 1024 * 1024
 
 
 def iota(shape, dim):
@@ -33,15 +38,18 @@
 
 def kernel(
     cfg,
-    og_ref,
-    ids_ref,
-    rw_ref,
+    og_hbm,
+    ids_hbm,
+    rw_hbm,
     sg_hbm,
     su_hbm,
     wg_hbm,
     wu_hbm,
     wd_hbm,
     out_ref,
+    og_ref,
+    ids_ref,
+    rw_ref,
     sg,
     su,
     wd,
@@ -99,14 +107,32 @@
 
     streams = ((1, 0, half), (1, 1, half - 1), (-1, 0, half - 1), (-1, 1, half))
 
+    firsts = [
+        pltpu.make_async_copy(ids_hbm, ids_ref, load_sem.at[5]),
+        pltpu.make_async_copy(rw_hbm, rw_ref, load_sem.at[6]),
+        pltpu.make_async_copy(og_hbm, og_ref, load_sem.at[7]),
+    ]
+    for first in firsts:
+        first.start()
+
     barrier = pltpu.get_barrier_semaphore()
 
+    side = math.isqrt(nodes)
+
+    def farthest(j):
+        return side // 2 + ((j + 1) // 2) * (1 - 2 * (j % 2))
+
+    def peer_at(i):
+        first = (node // side + farthest(i // side) + side) % side
+        second = (node % side + farthest(i % side) + side) % side
+        return first * side + second
+
     def greet(i, carry):
-        peer = (node + i) % nodes
+        peer = peer_at(i)
         pl.semaphore_signal(barrier, inc=1, device_id=(peer, local), device_id_type=MESH)
         return carry
 
-    lax.fori_loop(1, nodes, greet, 0)
+    lax.fori_loop(0, nodes - 1, greet, 0)
     for who in (right, left, sibling):
         pl.semaphore_signal(barrier, inc=1, device_id=(node, who), device_id_type=MESH)
 
@@ -120,17 +146,15 @@
     for load in loads:
         load.start()
 
+    for first in firsts:
+        first.wait()
     with jax.named_scope("fill_slots"):
-        idf = ids_ref[...].astype(F32)
+        idf = ids_ref[...].astype(F32).astype(BF16)
         gates = rw_ref[...].astype(F32)
         lane8 = iota((toks, LANE), 1)
-        tok8 = iota((toks, LANE), 0)
-        ids_lane = [
-            jnp.sum(
-                jnp.where(lane8 % toks == tok8, idf[:, j : j + 1], 0.0), axis=0, keepdims=True
-            ).astype(jnp.int32)
-            for j in range(picks)
-        ]
+        repeat = one_hot(lane8 % toks == iota((toks, LANE), 0))
+        ids_lanes = dot_nn(idf, repeat).astype(jnp.int32)
+        ids_lane = [ids_lanes[j : j + 1] for j in range(picks)]
         lane1 = iota((1, LANE), 1)
         slot_row = iota((slots, LANE), 0)
         hit = None
@@ -170,9 +194,9 @@
 
     pl.semaphore_wait(barrier, nodes - 1 + 3)
 
-    def to_node(src, dst, send_sem, recv_sem, c):
+    def to_node(src, dst, send_sem, recv_sem, c, lo=0, hi=nodes - 1):
         def go(i, carry):
-            peer = (node + i) % nodes
+            peer = peer_at(i)
             pltpu.make_async_remote_copy(
                 src_ref=src.at[c, peer],
                 dst_ref=dst.at[c, node],
@@ -183,7 +207,7 @@
             ).start()
             return carry
 
-        lax.fori_loop(1, nodes, go, 0)
+        lax.fori_loop(lo, hi, go, 0)
 
     def all_of(src, dst, send_sem, recv_sem, c):
         return pltpu.make_async_remote_copy(
@@ -195,60 +219,74 @@
             device_id_type=MESH,
         )
 
-    for c in range(CHUNKS):
-        to_node(tx, rx, out_send, out_recv, c)
-
-    def ag(c, st, s):
+    to_node(tx, rx, out_send, out_recv, 0)
+    to_node(tx, rx, out_send, out_recv, 1)
+
+    def cols(c, q):
+        lo = q * (tiles // PARTS) * LANE
+        hi = (q + 1) * (tiles // PARTS) * LANE
+        if q == PARTS - 1:
+            hi = width + (LANE if c == 0 else 0)
+        return pl.ds(lo, hi - lo)
+
+    def ag(c, st, s, q):
         way, h, _ = streams[st]
         return pltpu.make_async_remote_copy(
-            src_ref=xs[c].at[pos(-way * (s - 1)), 0, h],
-            dst_ref=xs[c].at[pos(-way * s), 0, h],
-            send_sem=ag_send.at[c, st, s - 1],
-            recv_sem=ag_recv.at[c, st, s - 1],
+            src_ref=xs[c].at[pos(-way * (s - 1)), 0, h, :, cols(c, q)],
+            dst_ref=xs[c].at[pos(-way * s), 0, h, :, cols(c, q)],
+            send_sem=ag_send.at[c, st, s - 1, q],
+            recv_sem=ag_recv.at[c, st, s - 1, q],
             device_id=(node, right if way > 0 else left),
             device_id_type=MESH,
         )
 
-    def to_sibling(c, p, h):
+    def to_sibling(c, p):
         return pltpu.make_async_remote_copy(
-            src_ref=xs[c].at[p, 0, h],
-            dst_ref=xs[c].at[p, 1, h],
-            send_sem=sib_send.at[c, p, h],
-            recv_sem=sib_recv.at[c, p, h],
+            src_ref=xs[c].at[p, 0],
+            dst_ref=xs[c].at[p, 1],
+            send_sem=sib_send.at[c, p],
+            recv_sem=sib_recv.at[c, p],
             device_id=(node, sibling),
             device_id_type=MESH,
         )
 
+    turns = (0, 3, 1, 2)
+
     def ag_start(c):
-        for st in range(4):
-            if streams[st][2] > 0:
-                ag(c, st, 1).start()
-        for h in range(2):
-            to_sibling(c, pos(0), h).start()
+        for q in range(PARTS):
+            for st in turns:
+                ag(c, st, 1, q).start()
+        to_sibling(c, pos(0)).start()
 
     def ag_step(c, s):
-        for st in (0, 3, 1, 2):
-            way, h, hops = streams[st]
-            if s <= hops:
-                ag(c, st, s).wait_recv()
-                if s < hops:
-                    ag(c, st, s + 1).start()
-                to_sibling(c, pos(-way * s), h).start()
+        for q in range(PARTS):
+            for st in turns:
+                way, h, hops = streams[st]
+                if s <= hops:
+                    ag(c, st, s, q).wait_recv()
+                    if s < hops:
+                        ag(c, st, s + 1, q).start()
+
+        for p in sorted({pos(s), pos(-s)}):
+            to_sibling(c, p).start()
 
     def sib_wait(c, ps):
         for p in ps:
-            for h in range(2):
-                to_sibling(c, p, h).wait_recv()
-
-    def fill_key():
+            to_sibling(c, p).wait_recv()
+
+    def key_constants():
+        first = one_hot(iota((SUB, LANE), 1) == 0)
+        owner = one_hot(iota((slots, LANE), 0) // SUB == iota((slots, LANE), 1))
+        below = one_hot(iota((LANE, slots), 0) <= iota((LANE, slots), 1) // SUB)
+        equal = one_hot(iota((LANE, slots), 0) == iota((LANE, slots), 1) // SUB)
+        return first, owner, below, equal
+
+    def fill_key(constants):
+        first, owner, below, equal = constants
         flat = rx[0].reshape(slots, LANE)
-        first = one_hot(iota((SUB, LANE), 1) == 0)
         lane_s = iota((SUB, slots), 1)
         flag = jnp.where(lane_s % SUB == SUB - 1, dot_nt(first, flat), 0.0).astype(BF16)
-        owner = one_hot(iota((slots, LANE), 0) // SUB == iota((slots, LANE), 1))
         by_node = dot_nn(flag, owner).astype(BF16)
-        below = one_hot(iota((LANE, slots), 0) <= iota((LANE, slots), 1) // SUB)
-        equal = one_hot(iota((LANE, slots), 0) == iota((LANE, slots), 1) // SUB)
         count = dot_nn(by_node, below)[0:1]
         filled = dot_nn(by_node, equal)[0:1]
         lane = iota((1, slots), 1)
@@ -325,42 +363,53 @@
     def chip_sum(c, p, h):
         return part[c, p, 0, h].astype(F32) + rsib[c, p, h].astype(F32)
 
-    def rs(c, st, s):
+    def part_cols(q):
+        return pl.ds(q * (width // PARTS), width // PARTS)
+
+    def rs(c, st, s, q):
         way = streams[st][0]
+        src = chain_start.at[c, st] if s == 1 else chain.at[c, st, s - 2]
         return pltpu.make_async_remote_copy(
-            src_ref=chain_start.at[c, st] if s == 1 else chain.at[c, st, s - 2],
-            dst_ref=chain.at[c, st, s - 1],
-            send_sem=rs_send.at[c, st, s - 1],
-            recv_sem=rs_recv.at[c, st, s - 1],
+            src_ref=src.at[:, part_cols(q)],
+            dst_ref=chain.at[c, st, s - 1, :, part_cols(q)],
+            send_sem=rs_send.at[c, st, s - 1, q],
+            recv_sem=rs_recv.at[c, st, s - 1, q],
             device_id=(node, right if way > 0 else left),
             device_id_type=MESH,
         )
 
-    def rs_start(c):
-        for p in range(3):
-            psib(c, p).wait_recv()
-        for st in (0, 3, 1, 2):
-            way, h, hops = streams[st]
-            chain_start[c, st] = chip_sum(c, pos(way * hops), h).astype(BF16)
-            rs(c, st, 1).start()
+    def chip_part(c, p, h, q):
+        return part[c, p, 0, h, :, part_cols(q)].astype(F32) + rsib[
+            c, p, h, :, part_cols(q)
+        ].astype(F32)
+
+    def rs_start(c, which=turns):
+        for q in range(PARTS):
+            for st in which:
+                way, h, hops = streams[st]
+                chain_start[c, st, :, part_cols(q)] = chip_part(c, pos(way * hops), h, q).astype(BF16)
+                rs(c, st, 1, q).start()
 
     def rs_step(c, s):
-        for st in (0, 3, 1, 2):
-            way, h, hops = streams[st]
-            if s < hops:
-                rs(c, st, s).wait_recv()
-                total = chain[c, st, s - 1].astype(F32) + chip_sum(c, pos(way * (hops - s)), h)
-                chain[c, st, s - 1] = total.astype(BF16)
-                rs(c, st, s + 1).start()
+        for q in range(PARTS):
+            for st in turns:
+                way, h, hops = streams[st]
+                if s < hops:
+                    rs(c, st, s, q).wait_recv()
+                    total = chain[c, st, s - 1, :, part_cols(q)].astype(F32)
+                    total = total + chip_part(c, pos(way * (hops - s)), h, q)
+                    chain[c, st, s - 1, :, part_cols(q)] = total.astype(BF16)
+                    rs(c, st, s + 1, q).start()
 
     def rs_finish(c):
         sums = []
         for h in range(2):
             total = chip_sum(c, pos(0), h)
             for st in range(4):
-                way, sh, hops = streams[st]
+                _, sh, hops = streams[st]
                 if sh == h:
-                    rs(c, st, hops).wait_recv()
+                    for q in range(PARTS):
+                        rs(c, st, hops, q).wait_recv()
                     total = total + chain[c, st, hops - 1].astype(F32)
             sums.append(total)
         total = jnp.concatenate(sums, axis=0).astype(BF16)
@@ -369,7 +418,9 @@
         back = dot_nn(pack_t[...], jnp.concatenate(stack, axis=0))
         tx2[c] = back.astype(BF16).reshape(nodes, SUB, LANE)
         rx2[c, node] = tx2[c, node]
-        to_node(tx2, rx2, back_send, back_recv, c)
+
+    def back_to_node(c, lo, hi):
+        to_node(tx2, rx2, back_send, back_recv, c, lo, hi)
 
     def combine(c, merge):
         all_of(tx2, rx2, back_send, back_recv, c).wait_recv()
@@ -379,9 +430,10 @@
                 k * toks : (k + 1) * toks
             ].astype(BF16)
 
+    constants = key_constants()
     all_of(tx, rx, out_send, out_recv, 0).wait_recv()
     with jax.named_scope("compact"):
-        key = fill_key()
+        key = fill_key(constants)
         pack = one_hot(iota((packed, slots), 0) == key)
         compact(0, pack)
     ag_start(0)
@@ -391,54 +443,68 @@
             pack_t[:, q * LANE : (q + 1) * LANE] = one_hot(
                 key_rows == iota((slots, LANE), 1) + q * LANE
             )
-    for load in loads:
-        load.wait()
-    ag_step(0, 1)
+    for s in range(1, C1_AFTER + 1):
+        ag_step(0, s)
     all_of(tx, rx, out_send, out_recv, 1).wait_recv()
     with jax.named_scope("compact"):
         compact(1, pack)
     ag_start(1)
+    for load in loads:
+        load.wait()
     last = len(order) - 1
 
     def pair(s):
         return (0, 1) if s == half else (pos(s), pos(-s) + 1) if s else (last, last + 1)
 
-    for s in range(1, half + 1):
-        if s < half:
-            ag_step(0, s + 1)
-        ag_step(1, s)
-        p0, p1 = pair(s - 1)
+    def hidden(s):
+        p0, p1 = pair(s)
         for c in range(CHUNKS):
             sib_wait(c, range(p0, p1))
             project(c, p0, p1)
         activate(p0, p1)
-    p0, p1 = pair(half)
-    for c in range(CHUNKS):
-        sib_wait(c, range(p0, p1))
-        project(c, p0, p1)
-    activate(p0, p1)
-
-    expand(0, 0, 3)
-    rs_start(0)
-    expand(1, 0, 3)
-    rs_start(1)
+
+    for s in range(1, half):
+        if s + C1_AFTER <= half:
+            ag_step(0, s + C1_AFTER)
+        ag_step(1, s)
+        hidden(s - 1)
     expand(0, 3, last + 1)
-    for p in range(3, last + 1):
+    if C1_AFTER == 0:
+        ag_step(0, half)
+    ag_step(1, half)
+    hidden(half - 1)
+    expand(0, 1, 3)
+    for p in range(1, 3):
         psib(0, p).wait_recv()
-    rs_step(0, 1)
-    expand(1, 3, last + 1)
-    for p in range(3, last + 1):
+    rs_start(0, (1, 2))
+    hidden(half)
+    expand(0, 0, 1)
+    for p in (0, *range(3, last + 1)):
+        psib(0, p).wait_recv()
+    rs_start(0, (0, 3))
+    expand(1, 0, last + 1)
+    for p in range(last + 1):
         psib(1, p).wait_recv()
-    rs_step(1, 1)
-    for s in range(2, half):
-        for c in range(CHUNKS):
-            rs_step(c, s)
-    for c in range(CHUNKS):
-        rs_finish(c)
+    if RS_LAG == 0:
+        rs_start(1)
+    for s in range(1, half):
+        rs_step(0, s)
+        if s == RS_LAG:
+            rs_start(1)
+        if s > RS_LAG:
+            rs_step(1, s - RS_LAG)
+    rs_finish(0)
+    cuts = [(nodes - 1) * i // (RS_LAG + 1) for i in range(RS_LAG + 2)]
+    back_to_node(0, cuts[0], cuts[1])
+    for i in range(RS_LAG):
+        rs_step(1, half - RS_LAG + i)
+        back_to_node(0, cuts[i + 1], cuts[i + 2])
+    rs_finish(1)
+    back_to_node(1, 0, nodes - 1)
     with jax.named_scope("merge_matrix"):
         spot = iota((LANE, nodes * SUB), 1)
         tok_row = one_hot(iota((LANE, toks), 0) % toks == iota((LANE, toks), 1))
-        ids_rows = dot_nn(tok_row, idf.astype(BF16)).astype(jnp.int32)
+        ids_rows = dot_nt(tok_row, idf).astype(jnp.int32)
         row_tile = iota((LANE, 1), 0) // toks
         hit = None
         for j in range(picks):
@@ -453,11 +519,11 @@
         all_of(tx2, rx2, back_send, back_recv, c).wait_send()
         for st in range(4):
             for s in range(1, streams[st][2] + 1):
-                ag(c, st, s).wait_send()
-                rs(c, st, s).wait_send()
+                for q in range(PARTS):
+                    ag(c, st, s, q).wait_send()
+                    rs(c, st, s, q).wait_send()
         for p in range(last + 1):
-            for h in range(2):
-                to_sibling(c, p, h).wait_send()
+            to_sibling(c, p).wait_send()
             psib(c, p).wait_send()
 
 
@@ -472,13 +538,15 @@
     sg = sg.reshape(2 * ring, rows, LANE)
     su = su.reshape(2 * ring, rows, LANE)
     in_vmem = pl.BlockSpec(memory_space=pltpu.VMEM)
-    anywhere = pl.BlockSpec(memory_space=pl.ANY)
     return pl.pallas_call(
         functools.partial(kernel, cfg),
         out_shape=jax.ShapeDtypeStruct(og.shape, BF16),
-        in_specs=[in_vmem] * 3 + [anywhere] * 5,
+        in_specs=[pl.BlockSpec(memory_space=pltpu.HBM)] * 8,
         out_specs=in_vmem,
         scratch_shapes=[
+            pltpu.VMEM(og.shape, BF16),
+            pltpu.VMEM(ids.shape[::-1], jnp.int32),
+            pltpu.VMEM(rw.shape, BF16),
             pltpu.VMEM(sg.shape, BF16),
             pltpu.VMEM(su.shape, BF16),
             pltpu.VMEM(wd.shape, BF16),
@@ -496,24 +564,24 @@
             pltpu.VMEM((CHUNKS, ring, 2, piece, width), BF16),
             pltpu.VMEM((CHUNKS, 4, piece, width), BF16),
             pltpu.VMEM((CHUNKS, 4, half, piece, width), BF16),
-            dma((5,)),
+            dma((8,)),
             dma((CHUNKS,)),
             dma((CHUNKS,)),
             dma((CHUNKS,)),
             dma((CHUNKS,)),
-            dma((CHUNKS, 4, half)),
-            dma((CHUNKS, 4, half)),
-            dma((CHUNKS, ring, 2)),
-            dma((CHUNKS, ring, 2)),
+            dma((CHUNKS, 4, half, PARTS)),
+            dma((CHUNKS, 4, half, PARTS)),
             dma((CHUNKS, ring)),
             dma((CHUNKS, ring)),
-            dma((CHUNKS, 4, half)),
-            dma((CHUNKS, 4, half)),
+            dma((CHUNKS, ring)),
+            dma((CHUNKS, ring)),
+            dma((CHUNKS, 4, half, PARTS)),
+            dma((CHUNKS, 4, half, PARTS)),
         ],
         compiler_params=pltpu.CompilerParams(
-            collective_id=0, has_side_effects=True, vmem_limit_bytes=48 * 1024 * 1024
+            collective_id=0, has_side_effects=True, vmem_limit_bytes=VMEM_BYTES
         ),
-    )(og, ids, rw, sg, su, wg, wu, wd)
+    )(og, ids.T, rw, sg, su, wg, wu, wd)
 
 
 def solution(mesh):

time: 110 us -> 101 us (0.918)
  local copies, waits for them, and re-layouts: 8.15 us -> 1.45 us
  Pallas kernels: 102 us -> 99 us
    unnamed x18 -> x1, local copies, waits for them, and re-layouts: 8.15 us -> 1.45 us
    pallas_call x1, Pallas kernels: 102 us -> 99 us  [layer(): pl.pallas_call(functools.partial(kernel, cfg), out_shape=jax.ShapeDtypeSt...]
where the time goes in v2:
time: 101 us; the launch traced here: 100 us
  Pallas kernels  99 us (98%)
  local copies, waits for them, and re-layouts  1.45 us (1%)
    pallas_call x1, Pallas kernels, layer(): pl.pallas_call(functools.partial(kernel, cfg), out_shape=jax.ShapeDtypeSt...  99 us

profile of v2, /device:TPU:1, one launch (start us, length us, event | category | flops | bytes accessed | tf_op | source)
XLA Modules:
  0.0 100.4 jit_solution(14176663847849470634)
XLA Ops:
  0.0 99.0 %shard_map.82 = bf16[8,3584]{1,0:T(8,128)(2,1)} custom-call(bf16[8,3584]{1,0:T(8,128)(2,1)} %og_hbm.1, s32[4,8]{1,0:T(4,128)} %bitcast.5, bf16[8,8]{1,0:T(8,128)(2,1)} %rw_hbm.1, bf16[16,32,128]{2,1,0:T(8,128)(2,1)} %bitcast.3, bf16[16,32,128]{2,1,0:T(8,128)(2,1)} %bitcast.4, bf16[3584,128]{1,0:T(8,128)(2,1)} %wg_hbm.1, bf16[3584,128]{1,0:T(8,128)(2,1)} %wu_hbm.1, ...), custom_call_target="tpu_custom_call" | custom-call | tf_op jit(solution)/shard_map/pallas_call | solution.py:541
  99.0 1.4 %copy.10 = bf16[8,3584]{1,0:T(8,128)(2,1)} copy(bf16[8,3584]{1,0:T(8,128)(2,1)} %shard_map.82) | data formatting | bytes 114688

commit v3 on v2

--- a/solution.py
+++ b/solution.py
@@ -468,7 +468,8 @@
             ag_step(0, s + C1_AFTER)
         ag_step(1, s)
         hidden(s - 1)
-    expand(0, 3, last + 1)
+    for c in range(CHUNKS):
+        expand(c, 3, last + 1)
     if C1_AFTER == 0:
         ag_step(0, half)
     ag_step(1, half)
@@ -482,14 +483,12 @@
     for p in (0, *range(3, last + 1)):
         psib(0, p).wait_recv()
     rs_start(0, (0, 3))
-    expand(1, 0, last + 1)
-    for p in range(last + 1):
-        psib(1, p).wait_recv()
-    if RS_LAG == 0:
-        rs_start(1)
+    expand(1, 0, 3)
     for s in range(1, half):
         rs_step(0, s)
         if s == RS_LAG:
+            for p in range(last + 1):
+                psib(1, p).wait_recv()
             rs_start(1)
         if s > RS_LAG:
             rs_step(1, s - RS_LAG)

time: 101 us -> 100 us (0.990)
  the two profiles are of different devices: /device:TPU:1 before, /device:TPU:16 now
where the time goes in v3:
time: 100 us
  Pallas kernels  98.7 us (99%)
  local copies, waits for them, and re-layouts  1.45 us (1%)
    pallas_call x1, Pallas kernels, layer(): pl.pallas_call(functools.partial(kernel, cfg), out_shape=jax.ShapeDtypeSt...  98.7 us

profile of v3, /device:TPU:16, one launch (start us, length us, event | category | flops | bytes accessed | tf_op | source)
XLA Modules:
  0.0 100.2 jit_solution(11647707292488989029)
XLA Ops:
  0.0 98.7 %shard_map.82 = bf16[8,3584]{1,0:T(8,128)(2,1)} custom-call(bf16[8,3584]{1,0:T(8,128)(2,1)} %og_hbm.1, s32[4,8]{1,0:T(4,128)} %bitcast.5, bf16[8,8]{1,0:T(8,128)(2,1)} %rw_hbm.1, bf16[16,32,128]{2,1,0:T(8,128)(2,1)} %bitcast.3, bf16[16,32,128]{2,1,0:T(8,128)(2,1)} %bitcast.4, bf16[3584,128]{1,0:T(8,128)(2,1)} %wg_hbm.1, bf16[3584,128]{1,0:T(8,128)(2,1)} %wu_hbm.1, ...), custom_call_target="tpu_custom_call" | custom-call | tf_op jit(solution)/shard_map/pallas_call | solution.py:540
  98.8 1.4 %copy.10 = bf16[8,3584]{1,0:T(8,128)(2,1)} copy(bf16[8,3584]{1,0:T(8,128)(2,1)} %shard_map.82) | data formatting | bytes 114688
